TPU v7x, 256 devices: a whole 4x4x8 slice. The times are simulated.
256 devices in a mesh: prow: 8 (over x, core), pcol: 32 (over y, z).
Axes of the slice: x: 4, y: 4, z: 8, core: 2. Of those that a mesh axis runs over, the one named last changes fastest.
Arguments:
- leaf_rhs: float32 [8192, 1024], P('prow'), may hold values from -6 to 6
- leaf_inverse: float32 [8192, 256], P(('prow', 'pcol')), may hold values from -0.375 to 0.375
- parent_rhs: float32 [32, 2048, 1024], P('pcol', 'prow'), may hold values from -6 to 6
- parent_inverse: float32 [32, 2048, 256], P('pcol', 'prow'), may hold values from -0.375 to 0.375
- factor: float32 [32, 2048, 8192], P('pcol', None, 'prow'), may hold values from -0.0234375 to 0.0234375
- tile_mask: int32 [32, 8, 32], P('pcol', None, 'prow'), may hold values from 0 to 1, as said below
Outputs:
- parent_solution: float32 [32, 2048, 1024], P('pcol', 'prow')
- leaf_solution: float32 [8192, 1024], P(('prow', 'pcol'))
Inputs may be any that keep to these rules, and one draw needn't show every extreme that they name: `tile_mask`: 1 marks a stored factor tile, 0 an absent one.
All inputs are finite; a program needn't handle non-finite values.
Results may differ from a plain program's by a relative error of at most 0.0001.
Values sent between devices are 32-bit elements; how exact they have to be, the bound alone decides.
A program may use at most 192 MiB of HBM per device.

v0:
```python
import jax
import jax.numpy as jnp
from jax import lax
from jax.sharding import PartitionSpec as P


def from_partner(shard, axis, bit):
    return lax.ppermute(shard, axis, [(i, i ^ 1 << bit) for i in range(lax.axis_size(axis))])


def body(leaf_rhs, leaf_inverse, parent_rhs, parent_inverse, factor, tile_mask):
    highest = lax.Precision.HIGHEST
    tile_size = parent_inverse.shape[2]
    rows_here = leaf_inverse.shape[0]
    leaf_rows = leaf_rhs.shape[0]
    per_row = leaf_rows // tile_size
    columns_rhs = leaf_rhs.shape[1]
    factor_rows = factor[0]
    mask_rows = jnp.repeat(tile_mask[0].astype(jnp.float32), tile_size, axis=0)
    grid_column = lax.axis_index("pcol")
    first_row = grid_column * rows_here
    leaf_pick = first_row // tile_size
    row_offset = first_row % tile_size
    contract_first = (((0,), (0,)), ((), ()))
    own_rhs = lax.dynamic_slice_in_dim(leaf_rhs, leaf_pick * tile_size, tile_size, 0)
    solved_rows = jnp.dot(leaf_inverse, own_rhs, precision=highest)
    leaf_forward = lax.all_gather(solved_rows, "pcol", axis=0, tiled=True)
    tile_slab = factor_rows
    weights_here = mask_rows
    summed = jnp.zeros((lax.axis_size("prow") * tile_size, columns_rhs), jnp.float32)
    for member in range(per_row):
        product = jnp.dot(
            tile_slab[:, member * tile_size : (member + 1) * tile_size],
            leaf_forward[member * tile_size : (member + 1) * tile_size],
            precision=highest,
        )
        summed = summed + weights_here[:, member : member + 1] * product
    update = lax.psum_scatter(summed, "prow", scatter_dimension=0, tiled=True)
    residue = parent_rhs[0] - update
    parent_forward = jnp.dot(parent_inverse[0], residue, precision=highest)
    parent_back = lax.dot_general(
        parent_inverse[0], parent_forward, contract_first, precision=highest
    )
    gathered = lax.all_gather(parent_back, "prow", axis=0, tiled=True)
    tile_slab = factor_rows
    weights_here = mask_rows
    fresh = []
    for member in range(per_row):
        weighted = weights_here[:, member : member + 1] * gathered
        fresh.append(
            lax.dot_general(
                tile_slab[:, member * tile_size : (member + 1) * tile_size],
                weighted,
                contract_first,
                precision=highest,
            )
        )
    leaf_update = jnp.concatenate(fresh, axis=0)
    update_rows = lax.psum_scatter(leaf_update, "pcol", scatter_dimension=0, tiled=True)
    remaining = solved_rows - update_rows
    collected = jnp.concatenate([remaining, leaf_inverse], axis=1)
    group_bits = (tile_size // rows_here).bit_length() - 1
    for level_bit in range(group_bits):
        partner = from_partner(collected, "pcol", level_bit)
        upper = grid_column >> level_bit & 1 == 1
        collected = jnp.where(
            upper,
            jnp.concatenate([partner, collected], axis=0),
            jnp.concatenate([collected, partner], axis=0),
        )
    block_remaining = collected[:, :columns_rhs]
    block_inverse = collected[:, columns_rhs:]
    inverse_columns = lax.dynamic_slice_in_dim(block_inverse, row_offset, rows_here, 1)
    leaf_out = lax.dot_general(inverse_columns, block_remaining, contract_first, precision=highest)
    return (parent_back[None], leaf_out)


def solution(mesh):
    placed = (
        P("prow", None),
        P(("prow", "pcol"), None),
        P("pcol", "prow", None),
        P("pcol", "prow", None),
        P("pcol", None, "prow"),
        P("pcol", None, "prow"),
    )
    return jax.shard_map(
        body,
        mesh=mesh,
        in_specs=placed,
        out_specs=(P("pcol", "prow", None), P(("prow", "pcol"), None)),
        check_vma=False,
    )
```

profile of v0, /device:TPU:2, one launch (start us, length us, event | category | flops | bytes accessed | tf_op | source)
XLA Modules:
  0.0 575.7 jit_solution(10073594695709928413)
XLA Ops:
  7.2 0.0 copy-start
  7.2 0.0 all-gather.3.cloned.1.call-start
  7.2 2.6 convolution_bitcast_fusion
  9.9 0.0 all-gather.3.cloned.1.call-update
  9.9 0.0 reduce-scatter.3.cloned.1.call-start
  9.9 0.7 convert_bitcast_fusion
  10.6 0.1 broadcast_bitcast_fusion
  10.8 85.2 %all-gather.3.cloned.1.call-done = f32[1024,1024]{1,0:T(8,128)} async-done(((f32[32,1024]{1,0:T(8,128)}), f32[1024,1024]{1,0:T(8,128)}) %all-gather.3.cloned.1.call-update) | async-done | bytes 4194320 | tf_op jit(solution)/shard_map/all_gather | solution.py:27
  96.0 0.0 copy-start.3
  96.0 9.3 %fusion.15 = f32[1024,2048]{0,1:T(8,128)S(1)} fusion(f32[2048,1024]{1,0:T(8,128)} %bitcast.37, f32[1024,1024]{1,0:T(8,128)} %all-gather.3.cloned.1.call-done), kind=kOutput, calls=%fused_computation.17 | convolution fusion | flops 6442450944 | bytes 11534336 | tf_op jit(solution)/shard_map/dot_general | solution.py:32
  105.3 0.0 copy-done.3
  105.3 0.0 copy-start.5
  105.3 10.6 %fusion.18 = f32[1024,2048]{0,1:T(8,128)} fusion(f32[2048,1024]{1,0:T(8,128)S(1)} %bitcast.43, f32[1024,1024]{1,0:T(8,128)} %all-gather.3.cloned.1.call-done), kind=kOutput, calls=%fused_computation.20 | convolution fusion | flops 6442450944 | bytes 11534336 | tf_op jit(solution)/shard_map/dot_general | solution.py:32
  115.9 0.0 copy-done.5
  115.9 9.0 %fusion.21 = f32[1024,2048]{0,1:T(8,128)} fusion(f32[2048,1024]{1,0:T(8,128)S(1)} %bitcast.44, f32[1024,1024]{1,0:T(8,128)S(1)} %copy-done.5), kind=kOutput, calls=%fused_computation.23 | convolution fusion | flops 6442450944 | bytes 11534336 | tf_op jit(solution)/shard_map/dot_general | solution.py:32
  124.8 15.1 %add_bitcast_fusion = f32[2048,1024]{1,0:T(8,128)} fusion(f32[1024,2048]{0,1:T(8,128)S(1)} %fusion.15, f32[1024,2048]{0,1:T(8,128)} %fusion.18, f32[1024,2048]{0,1:T(8,128)} %fusion.21, f32[2048]{0:T(1024)S(1)} %bitcast.54, f32[2048]{0:T(1024)S(1)} %bitcast.52, f32[2048]{0:T(1024)S(1)} %bitcast.50, f32[2048]{0:T(1024)S(1)} %bitcast.48, ...), kind=kOutput, calls=%fused_computation.8 | convolution fusion | flops 6457131008 | bytes 36732928 | tf_op jit(solution)/shard_map/dot_general | solution.py:32
  139.9 0.0 copy-start.7
  139.9 0.0 reduce-scatter.3.cloned.1.call-update
  139.9 0.3 all-gather.5.cloned.1.call-start
  140.2 49.7 %reduce-scatter.3.cloned.1.call-done = f32[256,1024]{1,0:T(8,128)} async-done(((f32[2048,1024]{1,0:T(8,128)}), f32[256,1024]{1,0:T(8,128)}) %reduce-scatter.3.cloned.1.call-update) | async-done | bytes 1048592 | tf_op jit(solution)/shard_map/reduce_scatter | solution.py:38
  189.9 0.0 copy-done
  189.9 0.0 copy-done.7
  189.9 3.0 fusion.49
  193.0 2.0 fusion.51
  194.9 0.0 all-gather.5.cloned.1.call-update
  194.9 0.0 reduce-scatter.5.cloned.1.call-start
  195.0 53.6 %all-gather.5.cloned.1.call-done = f32[2048,1024]{0,1:T(8,128)} async-done(((f32[256,1024]{0,1:T(8,128)}), f32[2048,1024]{0,1:T(8,128)}) %all-gather.5.cloned.1.call-update) | async-done | bytes 8388624 | tf_op jit(solution)/shard_map/all_gather | solution.py:44
  248.6 0.0 copy-start.2
  248.6 11.0 %fusion.38 = f32[256,1024]{1,0:T(8,128)S(1)} fusion(f32[2048,1024]{1,0:T(8,128)} %bitcast.39, f32[2048,1024]{0,1:T(8,128)} %all-gather.5.cloned.1.call-done, f32[2048]{0:T(1024)S(1)} %bitcast.55), kind=kOutput, calls=%fused_computation.28 | convolution fusion | flops 6444548096 | bytes 11542528 | tf_op jit(solution)/shard_map/dot_general | solution.py:51
  259.5 0.0 copy-done.2
  259.5 9.3 %fusion.33 = f32[256,1024]{1,0:T(8,128)S(1)} fusion(f32[2048,1024]{1,0:T(8,128)} %bitcast.40, f32[2048,1024]{0,1:T(8,128)S(1)} %copy-done.2, f32[2048]{0:T(1024)S(1)} %bitcast.53), kind=kOutput, calls=%fused_computation.27 | convolution fusion | flops 6444548096 | bytes 11542528 | tf_op jit(solution)/shard_map/dot_general | solution.py:51
  268.9 9.5 %fusion.28 = f32[256,1024]{1,0:T(8,128)S(1)} fusion(f32[2048,1024]{1,0:T(8,128)} %bitcast.41, f32[2048,1024]{0,1:T(8,128)S(1)} %copy-done.2, f32[2048]{0:T(1024)S(1)} %bitcast.51), kind=kOutput, calls=%fused_computation.26 | convolution fusion | flops 6444548096 | bytes 11542528 | tf_op jit(solution)/shard_map/dot_general | solution.py:51
  278.4 9.3 %fusion.23 = f32[256,1024]{1,0:T(8,128)S(1)} fusion(f32[2048,1024]{1,0:T(8,128)} %bitcast.42, f32[2048,1024]{0,1:T(8,128)S(1)} %copy-done.2, f32[2048]{0:T(1024)S(1)} %bitcast.49), kind=kOutput, calls=%fused_computation.25 | convolution fusion | flops 6444548096 | bytes 11542528 | tf_op jit(solution)/shard_map/dot_general | solution.py:51
  287.7 0.0 copy-start.6
  287.7 0.0 copy-start.8
  287.7 0.0 copy-start.4
  287.7 0.0 copy-start.1
  287.7 2.7 pad_maximum_fusion
  290.5 0.0 reduce-scatter.5.cloned.1.call-update
  290.5 222.2 %reduce-scatter.5.cloned.1.call-done = f32[32,1024]{1,0:T(8,128)} async-done(((f32[1024,1024]{1,0:T(8,128)}), f32[32,1024]{1,0:T(8,128)}) %reduce-scatter.5.cloned.1.call-update) | async-done | bytes 131088 | tf_op jit(solution)/shard_map/reduce_scatter | solution.py:59
  512.7 0.0 copy-done.6
  512.7 0.9 sub.12
  513.6 0.0 copy-done.8
  513.7 0.7 collective-permute-start
  514.3 4.7 collective-permute-done
  519.1 4.0 collective-permute-start.1
  523.1 22.6 %collective-permute-done.1 = f32[64,1280]{1,0:T(8,128)S(1)} collective-permute-done((f32[64,1280]{1,0:T(8,128)S(1)}, f32[64,1280]{1,0:T(8,128)S(1)}, u32[]{:S(2)}, u32[]{:S(2)}) %collective-permute-start.1) | collective-permute-done | bytes 327712 | tf_op jit(solution)/shard_map/ppermute | solution.py:8
  545.7 4.6 collective-permute-start.2
  550.3 0.0 copy-done.4
  550.3 1.3 copy.10
  551.6 15.8 %collective-permute-done.2 = f32[128,1280]{1,0:T(8,128)S(1)} collective-permute-done((f32[128,1280]{1,0:T(8,128)S(1)}, f32[128,1280]{1,0:T(8,128)S(1)}, u32[]{:S(2)}, u32[]{:S(2)}) %collective-permute-start.2) | collective-permute-done | bytes 655392 | tf_op jit(solution)/shard_map/ppermute | solution.py:8
  567.4 0.1 maximum_select_fusion
  567.6 1.4 fusion.43
  569.0 0.0 copy-done.1
  (6 shorter events, 0.1 us)
Async XLA Ops:
  7.2 182.7 %copy-start = (f32[1,256,256]{2,1,0:T(8,128)S(1)}, f32[1,256,256]{2,1,0:T(8,128)}, u32[]{:S(2)}) copy-start(f32[1,256,256]{2,1,0:T(8,128)} %param.9) | copy-start | bytes 786436
  7.2 88.8 %all-gather.3.cloned.1.call-start = ((), (), s32[]{:S(2)}) async-start(), calls=%async_computation.2 | async-start | bytes 4325376 | tf_op jit(solution)/shard_map/all_gather | solution.py:27
  9.9 180.0 %reduce-scatter.3.cloned.1.call-start = ((), (), s32[]{:S(2)}) async-start(), calls=%async_computation.3 | async-start | bytes 9437184 | tf_op jit(solution)/shard_map/reduce_scatter | solution.py:38
  96.0 9.3 %copy-start.3 = (f32[1,2048,1024]{2,1,0:T(8,128)S(1)}, f32[1,2048,1024]{2,1,0:T(8,128)}, u32[]{:S(2)}) copy-start(f32[1,2048,1024]{2,1,0:T(8,128)} %param.10) | copy-start | bytes 25165828
  105.3 10.6 %copy-start.5 = (f32[1024,1024]{1,0:T(8,128)S(1)}, f32[1024,1024]{1,0:T(8,128)}, u32[]{:S(2)}) copy-start(f32[1024,1024]{1,0:T(8,128)} %all-gather.3.cloned.1.call-done) | copy-start | bytes 12582916
  139.9 50.0 %copy-start.7 = (f32[1,256,1024]{2,1,0:T(8,128)S(1)}, f32[1,256,1024]{2,1,0:T(8,128)}, u32[]{:S(2)}) copy-start(f32[1,256,1024]{2,1,0:T(8,128)} %param.8) | copy-start | bytes 3145732
  139.9 108.6 %all-gather.5.cloned.1.call-start = ((), (), s32[]{:S(2)}) async-start(), calls=%async_computation.4 | async-start | bytes 9437184 | tf_op jit(solution)/shard_map/all_gather | solution.py:44
  194.9 317.8 %reduce-scatter.5.cloned.1.call-start = ((), (), s32[]{:S(2)}) async-start(), calls=%async_computation.5 | async-start | bytes 4325376 | tf_op jit(solution)/shard_map/reduce_scatter | solution.py:59
  248.6 11.0 %copy-start.2 = (f32[2048,1024]{0,1:T(8,128)S(1)}, f32[2048,1024]{0,1:T(8,128)}, u32[]{:S(2)}) copy-start(f32[2048,1024]{0,1:T(8,128)} %all-gather.5.cloned.1.call-done) | copy-start | bytes 25165828
  287.7 225.0 %copy-start.6 = (f32[32,1024]{1,0:T(8,128)S(1)}, f32[32,1024]{1,0:T(8,128)}, u32[]{:S(2)}) copy-start(f32[32,1024]{1,0:T(8,128)} %convolution_bitcast_fusion) | copy-start | bytes 393220
  287.7 225.9 %copy-start.8 = (f32[32,256]{1,0:T(8,128)S(1)}, f32[32,256]{1,0:T(8,128)}, u32[]{:S(2)}) copy-start(f32[32,256]{1,0:T(8,128)} %param.7) | copy-start | bytes 98308
  287.7 262.6 %copy-start.4 = (f32[1024,256]{1,0:T(8,128)S(1)}, f32[1024,256]{1,0:T(8,128)}, u32[]{:S(2)}) copy-start(f32[1024,256]{1,0:T(8,128)} %fusion.51) | copy-start | bytes 3145732
  287.7 281.3 %copy-start.1 = (f32[1,256,256]{2,1,0:T(8,128)S(1)}, f32[1,256,256]{2,1,0:T(8,128)}, u32[]{:S(2)}) copy-start(f32[1,256,256]{2,1,0:T(8,128)} %param.9) | copy-start | bytes 786436
  513.7 5.4 collective-permute-start
  519.1 26.6 %collective-permute-start.1 = (f32[64,1280]{1,0:T(8,128)S(1)}, f32[64,1280]{1,0:T(8,128)S(1)}, u32[]{:S(2)}, u32[]{:S(2)}) collective-permute-start(f32[64,1280]{1,0:T(8,128)S(1)} %maximum_select_fusion.2), channel_id=1, source_target_pairs={{0,2},{1,3},{2,0},{3,1},{4,6},{5,7},{6,4},{7,5},{8,10},{9,11},{10,... | collective-permute-start | bytes 983048 | tf_op jit(solution)/shard_map/ppermute | solution.py:8
  545.7 21.7 %collective-permute-start.2 = (f32[128,1280]{1,0:T(8,128)S(1)}, f32[128,1280]{1,0:T(8,128)S(1)}, u32[]{:S(2)}, u32[]{:S(2)}) collective-permute-start(f32[128,1280]{1,0:T(8,128)S(1)} %maximum_select_fusion.1), channel_id=1, source_target_pairs={{0,4},{1,5},{2,6},{3,7},{4,0},{5,1},{6,2},{7,3},{8,12},{9,13},{10,... | collective-permute-start | bytes 1966088 | tf_op jit(solution)/shard_map/ppermute | solution.py:8
Sparse Core Ops, SparseCore 0:
  11.2 84.7 all-gather.2
  140.0 49.8 reduce-scatter.2
  195.1 53.4 all-gather.4
  290.6 222.0 reduce-scatter.4
where the time goes:
time: 582 us; the launch traced here: 576 us
  waiting for transfers between devices  454 us (78%)
  matrix products  92 us (16%)
  between operations  14.2 us (2%)
  starting transfers between devices  9.58 us (2%)
    reduce_scatter x1, waiting for transfers between devices, body(): lax.psum_scatter(leaf_update, 'pcol', scatter_dimension=0, tiled=True)  222 us
    all_gather x1, waiting for transfers between devices, body(): leaf_forward = lax.all_gather(solved_rows, 'pcol', axis=0, tiled=True)  85.2 us
    all_gather x1, waiting for transfers between devices, body(): gathered = lax.all_gather(parent_back, 'prow', axis=0, tiled=True)  53.6 us
    reduce_scatter x1, waiting for transfers between devices, body(): update = lax.psum_scatter(summed, 'prow', scatter_dimension=0, tiled=True)  49.7 us
    dot_general x4, matrix products, body(): jnp.dot(tile_slab[:, member * tile_size:(member + 1) * tile_size], leaf_f...  43.9 us
    ppermute x3, waiting for transfers between devices, from_partner(): lax.ppermute(shard, axis, [(i, i ^ 1 << bit) for i in range(lax.axis_size...  43.2 us
    dot_general x4, matrix products, body(): lax.dot_general(tile_slab[:, member * tile_size:(member + 1) * tile_size]...  39.1 us
  transfers between devices with their start and end apart: 7, of which 7 were waited for; matrix products, arithmetic and copies ran while one was open for 0% of the time, Pallas kernels for 0%

commit v1 on v0

v1 whole, which is shorter than its diff:
```python
import jax
import jax.numpy as jnp
from jax import lax
from jax.experimental import pallas as pl
from jax.experimental.pallas import tpu as pltpu
from jax.sharding import PartitionSpec as P

MESH = pl.DeviceIdType.MESH
F32 = jnp.float32
BF16 = jnp.bfloat16
BS = 256
W = 128
N = 8
HB = BS // 2
ROWS = 32

(PAIR, XA, XB, MB, MA, PA, PB, GP, GM, GC, HA, HBK, FM, FP, FO, YXA, YXB, YMB, YMA, YPA, YPB, Z1) = range(22)
KINDS = Z1 + 7


def split(v):
    hi = v.astype(BF16)
    return hi, (v - hi.astype(F32)).astype(BF16)


def dot(a, b):
    return jnp.dot(a, b, preferred_element_type=F32)


def pair_of(v):
    return jnp.concatenate(split(v), axis=1)


def dot2(a, b):
    r = dot(a, b)
    return r[:, :W] + r[:, W:]


def dot1(a, b):
    return dot2(a, jnp.concatenate([b, b], axis=0))


ORDER = (
    ("forward", 0), ("opposite", 6), ("relay", 5), ("stage1", 0), ("z_send", 10),
    ("y_stage2", 8), ("solve", 3), ("finish", 13), ("stage2", 1), ("backward", 6),
)


def kernel(
    mask_in, rhs, inv, prhs, pinv, fac, out_p, out_l,
    f2, ft2, s_all, t_all, u_all, pair, xa, xb, ym, yp, yxa, yxb, yym, yyp, zr,
    inv_all, i2, it2, l2, s2, res, p2, pt2, d_all, mask,
    load_sem, out_sem, a_send, a_recv, send, recv,
):
    p = lax.axis_index("prow")
    q = lax.axis_index("pcol")
    x, k = p // 2, lax.rem(p, 2)
    y, z = q // 8, lax.rem(q, 8)
    xp, xm, xo = lax.rem(x + 1, 4), lax.rem(x + 3, 4), lax.rem(x + 2, 4)
    yp_i, ym_i, yo = lax.rem(y + 1, 4), lax.rem(y + 3, 4), lax.rem(y + 2, 4)
    dev_c = (x * 2 + 1 - k, q)
    dev_xp, dev_xm = (xp * 2 + k, q), (xm * 2 + k, q)
    dev_yp, dev_ym = (p, yp_i * 8 + z), (p, ym_i * 8 + z)

    def z_at(j):
        return lax.rem(z + j, 8)

    def dev_z(j):
        return (p, y * 8 + z_at(j))

    def dev_y(j):
        return (p, lax.rem(y + j, 4) * 8 + z)

    lo, up = pl.ds(0, HB), pl.ds(HB, HB)
    own = k * 4

    def rows(at, start=0, size=BS):
        return pl.ds(pl.multiple_of(at * BS + start, HB), size)

    def copy(kind, t):
        def go(src, dst, dev):
            return pltpu.make_async_remote_copy(
                src_ref=src, dst_ref=dst, send_sem=send.at[t, kind], recv_sem=recv.at[t, kind],
                device_id=dev, device_id_type=MESH,
            )

        if kind == PAIR:
            return go(u_all.at[t, 1 - k], pair.at[t], dev_c)
        if kind == XA:
            return go(u_all.at[t, k, rows(xo, 0, HB)], xa.at[t], dev_xp)
        if kind == XB:
            return go(u_all.at[t, k, rows(xo, HB, HB)], xb.at[t], dev_xm)
        if kind == MB:
            return go(u_all.at[t, k, rows(xp, HB, HB)], ym.at[t, up], dev_xp)
        if kind == MA:
            return go(u_all.at[t, k, rows(xp, 0, HB)], ym.at[t, lo], dev_xp)
        if kind == PA:
            return go(u_all.at[t, k, rows(xm, 0, HB)], yp.at[t, lo], dev_xm)
        if kind == PB:
            return go(u_all.at[t, k, rows(xm, HB, HB)], yp.at[t, up], dev_xm)
        if kind in (GP, GM, GC):
            ref = s_all.at[t, own + x]
            return go(ref, ref, {GP: dev_xp, GM: dev_xm, GC: dev_c}[kind])
        if kind == HA:
            ref = s_all.at[t, own + xm, lo]
            return go(ref, ref, dev_xp)
        if kind == HBK:
            ref = s_all.at[t, own + xp, up]
            return go(ref, ref, dev_xm)
        if kind in (FM, FP, FO):
            ref = s_all.at[t, own + {FM: xm, FP: xp, FO: xo}[kind]]
            return go(ref, ref, dev_c)
        if kind == YXA:
            return go(t_all.at[t, yo, lo], yxa.at[t], dev_yp)
        if kind == YXB:
            return go(t_all.at[t, yo, up], yxb.at[t], dev_ym)
        if kind == YMB:
            return go(t_all.at[t, yp_i, up], yym.at[t, up], dev_yp)
        if kind == YMA:
            return go(t_all.at[t, yp_i, lo], yym.at[t, lo], dev_yp)
        if kind == YPA:
            return go(t_all.at[t, ym_i, lo], yyp.at[t, lo], dev_ym)
        if kind == YPB:
            return go(t_all.at[t, ym_i, up], yyp.at[t, up], dev_ym)
        j = kind - Z1 + 1
        return go(t_all.at[t, y, pl.ds(z_at(j) * ROWS, ROWS)], zr.at[t, j - 1], dev_z(j))

    def start(t, *kinds):
        for kind in kinds:
            copy(kind, t).start()

    def arrived(t, *kinds):
        for kind in kinds:
            copy(kind, t).wait_recv()

    def load_f(i):
        return pltpu.make_async_copy(
            fac.at[:, :, pl.ds(i * W, W)], s_all.at[i], load_sem.at[i]
        )

    def load_r(t):
        return pltpu.make_async_copy(
            rhs.at[:, :, pl.ds(t * W, W)], t_all.at[t], load_sem.at[N + t]
        )

    def load_p(t):
        return pltpu.make_async_copy(
            prhs.at[:, pl.ds(t * W, W)], res.at[t], load_sem.at[2 * N + t]
        )

    load_m = pltpu.make_async_copy(mask_in, mask, load_sem.at[3 * N])
    load_m.start()
    for i in range(N):
        load_f(i).start()
    for t in range(N):
        load_r(t).start()
    for t in range(N):
        load_p(t).start()

    barrier = pltpu.get_barrier_semaphore()
    others = [dev_c, dev_xp, dev_xm]
    others += [dev_y(j) for j in range(1, 4)] + [dev_z(j) for j in range(1, 8)]
    for dev in others:
        pl.semaphore_signal(barrier, inc=1, device_id=dev, device_id_type=MESH)
    mine = pl.ds(pl.multiple_of(z * ROWS, ROWS), ROWS)
    inv_all[y, mine, :] = inv[...]
    pl.semaphore_wait(barrier, len(others))

    def piece(j, way):
        at = pl.ds(pl.multiple_of(lax.rem(z + 8 - j, 8) * ROWS, ROWS), ROWS)
        ref = inv_all.at[y, at]
        return pltpu.make_async_remote_copy(
            src_ref=ref, dst_ref=ref, send_sem=a_send.at[j, way], recv_sem=a_recv.at[j, way],
            device_id=dev_y(way) if way else dev_z(j), device_id_type=MESH,
        )

    def over_y(j):
        for way in (1, 3, 2):
            piece(j, way).start()

    def over_z(j):
        return pltpu.make_async_remote_copy(
            src_ref=inv_all.at[y, mine], dst_ref=inv_all.at[y, mine],
            send_sem=a_send.at[j, 0], recv_sem=a_recv.at[j, 0],
            device_id=dev_z(j), device_id_type=MESH,
        )

    for j in (1, 7, 2, 6, 3, 5, 4):
        over_z(j).start()
    over_y(0)

    def tiles(i):
        load_f(2 * i).wait()
        load_f(2 * i + 1).wait()

        @pl.loop(0, 8)
        def _(s):
            r = lax.rem(s, 4) * 2 + s // 4
            v = jnp.concatenate([s_all[2 * i, r], s_all[2 * i + 1, r]], axis=1)
            v = v * mask[0, r, i].astype(F32)
            here = rows(lax.rem(s, 4))
            hi, low = split(v)
            f2[s // 4, here, i * BS : (i + 1) * BS] = hi
            f2[s // 4, here, (4 + i) * BS : (5 + i) * BS] = low
            hi, low = split(v.T)
            half = slice(i % 2 * BS, (i % 2 + 1) * BS)
            ft2[i // 2, half, rows(s)] = hi
            ft2[i // 2, half, rows(8 + s)] = low

    load_m.wait()
    tiles(0)
    for j in (1, 7):
        over_z(j).wait_recv()
        over_y(j)
    tiles(1)
    for j in (2, 6, 3, 5):
        over_z(j).wait_recv()
        over_y(j)
    v = pinv[...]
    p2[...] = pair_of(v)
    pt2[...] = pair_of(v.T)
    over_z(4).wait_recv()
    over_y(4)
    tiles(2)
    tiles(3)
    for t in range(N):
        load_r(t).wait()
        load_p(t).wait()
    for j in range(8):
        for way in (1, 2, 3):
            piece(j, way).wait_recv()

    @pl.loop(0, 4)
    def _(i):
        v = inv_all[i]
        i2[i] = pair_of(v)
        it2[i] = pair_of(v.T)

    def forward(t):
        @pl.loop(0, 4)
        def _(i):
            b = pair_of(dot1(i2[i], pair_of(t_all[t, i])))
            l2[rows(i), :] = b
            l2[rows(4 + i), :] = b

        d_all[t] = dot1(it2[y, mine], l2[rows(y), :])
        u_all[t, 1 - k] = dot2(f2[1 - k], l2[...])
        start(t, PAIR)
        u_all[t, k] = dot2(f2[k], l2[...])

    def add(ref, at, other):
        ref[at] = ref[at] + other

    def stage1(t):
        arrived(t, PAIR)
        u, got = u_all.at[t, k], pair.at[t]
        add(u, rows(xo), got[rows(xo)])
        start(t, XA, XB)
        add(u, rows(xp), got[rows(xp)])
        add(u, rows(xm), got[rows(xm)])
        start(t, MB, PA)
        add(u, rows(x), got[rows(x)])

    def stage2(t):
        arrived(t, XA)
        add(u_all.at[t, k], rows(xp, 0, HB), xa[t])
        start(t, MA)
        arrived(t, XB)
        add(u_all.at[t, k], rows(xm, HB, HB), xb[t])
        start(t, PB)

    def keep(t):
        return pltpu.make_async_copy(s_all.at[t, own + x], out_p.at[:, pl.ds(t * W, W)], out_sem.at[t])

    def solve(t):
        arrived(t, MA, MB, PA, PB)
        v = res[t] - ((u_all[t, k, rows(x)] + ym[t]) + yp[t])
        v = dot1(p2[...], pair_of(v))
        s_all[t, own + x] = dot1(pt2[...], pair_of(v))
        start(t, GP, GM, GC)
        keep(t).start()

    def relay(t):
        arrived(t, GP)
        start(t, HA, FM)
        arrived(t, GM)
        start(t, HBK, FP)

    def opposite(t):
        arrived(t, HA, HBK)
        start(t, FO)

    def backward(t):
        arrived(t, GC, FM, FP, FO)

        @pl.loop(0, 8)
        def _(s):
            b = pair_of(s_all[t, s])
            s2[rows(s), :] = b
            s2[rows(8 + s), :] = b

        @pl.loop(0, 2)
        def _(i):
            v = dot2(ft2[i], s2[...])
            t_all[t, 2 * i] = dot1(it2[2 * i], pair_of(v[:BS]))
            t_all[t, 2 * i + 1] = dot1(it2[2 * i + 1], pair_of(v[BS:]))

        start(t, YXA, YXB, YMB, YPA)

    def y_stage2(t):
        arrived(t, YXA)
        t_all[t, yp_i, lo] = t_all[t, yp_i, lo] + yxa[t]
        start(t, YMA)
        arrived(t, YXB)
        t_all[t, ym_i, up] = t_all[t, ym_i, up] + yxb[t]
        start(t, YPB)

    def z_send(t):
        arrived(t, YMA, YMB, YPA, YPB)
        t_all[t, y] = (t_all[t, y] + yym[t]) + yyp[t]
        start(t, *range(Z1, Z1 + 7))

    def finish(t):
        arrived(t, *range(Z1, Z1 + 7))
        total = t_all[t, y, mine]
        for j in range(7):
            total = total + zr[t, j]
        out_l[:, pl.ds(pl.multiple_of(t * W, W), W)] = d_all[t] - total

    stages = dict(
        forward=forward, stage1=stage1, stage2=stage2, solve=solve, relay=relay, opposite=opposite,
        backward=backward, y_stage2=y_stage2, z_send=z_send, finish=finish,
    )

    @pl.loop(0, N + max(lag for _, lag in ORDER))
    def _(step):
        for name, lag in ORDER:
            t = step - lag

            @pl.when(jnp.logical_and(t >= 0, t < N))
            def _():
                stages[name](t)

    for j in range(8):
        for way in range(4):
            if j or way:
                (piece(j, way) if way else over_z(j)).wait_send()

    @pl.loop(0, N)
    def _(t):
        keep(t).wait()
        for kind in range(KINDS):
            copy(kind, t).wait_send()


def body(leaf_rhs, leaf_inverse, parent_rhs, parent_inverse, factor, tile_mask):
    vmem = pl.BlockSpec(memory_space=pltpu.VMEM)
    hbm = pl.BlockSpec(memory_space=pl.ANY)
    f32, b16 = (lambda *s: pltpu.VMEM(s, F32)), (lambda *s: pltpu.VMEM(s, BF16))
    dma = lambda *s: pltpu.SemaphoreType.DMA(s)
    solved, leaf = pl.pallas_call(
        kernel,
        out_shape=(
            jax.ShapeDtypeStruct((BS, N * W), F32),
            jax.ShapeDtypeStruct((ROWS, N * W), F32),
        ),
        in_specs=[hbm, hbm, vmem, hbm, vmem, hbm],
        out_specs=(hbm, vmem),
        scratch_shapes=[
            b16(2, 4 * BS, 8 * BS),
            b16(2, 2 * BS, 16 * BS),
            f32(N, 8, BS, W),
            f32(N, 4, BS, W),
            f32(N, 2, 4 * BS, W),
            f32(N, 4 * BS, W),
            f32(N, HB, W), f32(N, HB, W),
            f32(N, BS, W), f32(N, BS, W),
            f32(N, HB, W), f32(N, HB, W),
            f32(N, BS, W), f32(N, BS, W),
            f32(N, 7, ROWS, W),
            f32(4, BS, BS),
            b16(4, BS, 2 * BS), b16(4, BS, 2 * BS),
            b16(8 * BS, 2 * W),
            b16(16 * BS, 2 * W),
            f32(N, BS, W),
            b16(BS, 2 * BS), b16(BS, 2 * BS),
            f32(N, ROWS, W),
            pltpu.SMEM((1, 8, 4), jnp.int32),
            dma(3 * N + 1), dma(N), dma(8, 4), dma(8, 4), dma(N, KINDS), dma(N, KINDS),
        ],
        compiler_params=pltpu.CompilerParams(
            collective_id=0, has_side_effects=True, vmem_limit_bytes=63 * 2**20
        ),
    )(
        tile_mask,
        leaf_rhs.reshape(4, BS, N * W),
        leaf_inverse,
        parent_rhs[0],
        parent_inverse[0],
        factor[0].reshape(8, BS, 4 * BS),
    )
    return solved[None], leaf


def solution(mesh):
    placed = (
        P("prow", None),
        P(("prow", "pcol"), None),
        P("pcol", "prow", None),
        P("pcol", "prow", None),
        P("pcol", None, "prow"),
        P("pcol", None, "prow"),
    )
    return jax.shard_map(
        body,
        mesh=mesh,
        in_specs=placed,
        out_specs=(P("pcol", "prow", None), P(("prow", "pcol"), None)),
        check_vma=False,
    )
```

time: 582 us -> 144 us (0.25); the launches traced: 576 us -> 144 us
  waiting for transfers between devices: 454 us -> 0 us
  Pallas kernels: 0 us -> 138 us
  matrix products: 92 us -> 0 us
  between operations: 14.2 us -> 0.64 us
  starting transfers between devices: 9.58 us -> 0 us
    reduce_scatter x2 -> x0, waiting for transfers between devices: 272 us -> none  [the longest x1 222 us: body(): lax.psum_scatter(leaf_update, 'pcol', scatter_dimension=0, tiled=True)]
    all_gather x2 -> x0, waiting for transfers between devices: 139 us -> none  [the longest x1 85.2 us: body(): leaf_forward = lax.all_gather(solved_rows, 'pcol', axis=0, tiled=True)]
    pallas_call x0 -> x1, Pallas kernels: none -> 138 us  [body(): pl.pallas_call(kernel, out_shape=(jax.ShapeDtypeStruct((BS, N * W), F32),...]
    dot_general x12 -> x0, matrix products: 92 us -> none  [the longest x4 43.9 us: body(): jnp.dot(tile_slab[:, member * tile_size:(member + 1) * tile_size], leaf_f...]
    ppermute x3 -> x0, waiting for transfers between devices: 43.2 us -> none  [from_partner(): lax.ppermute(shard, axis, [(i, i ^ 1 << bit) for i in range(lax.axis_size...]
    ppermute x3 -> x0, starting transfers between devices: 9.2 us -> none  [from_partner(): lax.ppermute(shard, axis, [(i, i ^ 1 << bit) for i in range(lax.axis_size...]
  transfers between devices with their start and end apart: 7 -> 0, of which waited for: 7 -> 0; matrix products, arithmetic and copies ran while one was open for 0% -> 0% of each run, Pallas kernels for 0% -> 0%
where the time goes in v1:
time: 144 us
  Pallas kernels  138 us (96%)
  local copies, waits for them, and re-layouts  5.22 us (4%)
    pallas_call x1, Pallas kernels, body(): pl.pallas_call(kernel, out_shape=(jax.ShapeDtypeStruct((BS, N * W), F32),...  138 us
    unnamed x3, local copies, waits for them, and re-layouts  5.22 us

profile of v1, /device:TPU:2, one launch (start us, length us, event | category | flops | bytes accessed | tf_op | source)
XLA Modules:
  0.0 143.7 jit_solution(4052500223173894502)
XLA Ops:
  0.6 1.3 copy.8.mask_in
  2.0 137.8 %shard_map.77 = (f32[256,1024]{1,0:T(8,128)}, f32[32,1024]{1,0:T(8,128)}) custom-call(s32[1,8,4]{2,1,0:T(8,128)} %copy.8.mask_in, f32[4,256,1024]{2,1,0:T(8,128)} %bitcast.6, f32[32,256]{1,0:T(8,128)} %inv.1, f32[256,1024]{1,0:T(8,128)} %bitcast.7, f32[256,256]{1,0:T(8,128)} %bitcast.9, f32[8,256,1024]{2,1,0:T(8,128)} %bitcast.5), custom_call_target="tpu_custom_call" | custom-call | tf_op jit(solution)/shard_map/pallas_call | solution.py:361
  139.8 2.3 %copy.11 = f32[1,256,1024]{2,1,0:T(8,128)} copy(f32[1,256,1024]{2,1,0:T(8,128)} %bitcast.8) | data formatting | bytes 2097152
  142.1 1.6 %copy.12 = f32[32,1024]{1,0:T(8,128)} copy(f32[32,1024]{1,0:T(8,128)} %get-tuple-element.9) | data formatting | bytes 262144

commit v2 on v1

--- a/solution.py
+++ b/solution.py
@@ -197,7 +197,7 @@
         def _(s):
             r = lax.rem(s, 4) * 2 + s // 4
             v = jnp.concatenate([s_all[2 * i, r], s_all[2 * i + 1, r]], axis=1)
-            v = v * mask[0, r, i].astype(F32)
+            v = v * mask[0, i, r].astype(F32)
             here = rows(lax.rem(s, 4))
             hi, low = split(v)
             f2[s // 4, here, i * BS : (i + 1) * BS] = hi
@@ -244,9 +244,14 @@
             l2[rows(4 + i), :] = b
 
         d_all[t] = dot1(it2[y, mine], l2[rows(y), :])
-        u_all[t, 1 - k] = dot2(f2[1 - k], l2[...])
-        start(t, PAIR)
-        u_all[t, k] = dot2(f2[k], l2[...])
+        @pl.loop(0, 2)
+        def _(n):
+            core = lax.rem(1 - k + n, 2)
+            u_all[t, core] = dot2(f2[core], l2[...])
+
+            @pl.when(n == 0)
+            def _():
+                start(t, PAIR)
 
     def add(ref, at, other):
         ref[at] = ref[at] + other
@@ -326,6 +331,9 @@
         for j in range(7):
             total = total + zr[t, j]
         out_l[:, pl.ds(pl.multiple_of(t * W, W), W)] = d_all[t] - total
+        keep(t).wait()
+        for kind in range(KINDS):
+            copy(kind, t).wait_send()
 
     stages = dict(
         forward=forward, stage1=stage1, stage2=stage2, solve=solve, relay=relay, opposite=opposite,
@@ -346,11 +354,10 @@
             if j or way:
                 (piece(j, way) if way else over_z(j)).wait_send()
 
-    @pl.loop(0, N)
-    def _(t):
-        keep(t).wait()
-        for kind in range(KINDS):
-            copy(kind, t).wait_send()
+
+def hand_on(solved, leaf, out_p, out_l):
+    out_p[...] = solved[...]
+    out_l[...] = leaf[...]
 
 
 def body(leaf_rhs, leaf_inverse, parent_rhs, parent_inverse, factor, tile_mask):
@@ -385,20 +392,29 @@
             f32(N, BS, W),
             b16(BS, 2 * BS), b16(BS, 2 * BS),
             f32(N, ROWS, W),
-            pltpu.SMEM((1, 8, 4), jnp.int32),
+            pltpu.SMEM((1, 4, 8), jnp.int32),
             dma(3 * N + 1), dma(N), dma(8, 4), dma(8, 4), dma(N, KINDS), dma(N, KINDS),
         ],
         compiler_params=pltpu.CompilerParams(
             collective_id=0, has_side_effects=True, vmem_limit_bytes=63 * 2**20
         ),
     )(
-        tile_mask,
+        jnp.swapaxes(tile_mask, 1, 2),
         leaf_rhs.reshape(4, BS, N * W),
         leaf_inverse,
         parent_rhs[0],
         parent_inverse[0],
         factor[0].reshape(8, BS, 4 * BS),
     )
+    solved, leaf = pl.pallas_call(
+        hand_on,
+        out_shape=(
+            jax.ShapeDtypeStruct((BS, N * W), F32),
+            jax.ShapeDtypeStruct((ROWS, N * W), F32),
+        ),
+        in_specs=[vmem, vmem],
+        out_specs=(vmem, vmem),
+    )(solved, leaf)
     return solved[None], leaf
 
 

time: 144 us -> 135 us (0.938)
  local copies, waits for them, and re-layouts: 5.22 us -> 0 us
  Pallas kernels: 138 us -> 134 us
    pallas_call x1, Pallas kernels: 138 us -> 132 us  [body(): pl.pallas_call(kernel, out_shape=(jax.ShapeDtypeStruct((BS, N * W), F32),...]
    unnamed x3 -> x0, local copies, waits for them, and re-layouts: 5.22 us -> none
    pallas_call x0 -> x1, Pallas kernels: none -> 2.3 us  [body(): pl.pallas_call(hand_on, out_shape=(jax.ShapeDtypeStruct((BS, N * W), F32)...]
where the time goes in v2:
time: 135 us
  Pallas kernels  134 us (99%)
    pallas_call x1, Pallas kernels, body(): pl.pallas_call(kernel, out_shape=(jax.ShapeDtypeStruct((BS, N * W), F32),...  132 us

profile of v2, /device:TPU:2, one launch (start us, length us, event | category | flops | bytes accessed | tf_op | source)
XLA Modules:
  0.0 134.6 jit_solution(14388223520847507452)
XLA Ops:
  0.6 131.7 %shard_map.77 = (f32[256,1024]{1,0:T(8,128)}, f32[32,1024]{1,0:T(8,128)}) custom-call(s32[1,4,8]{2,1,0:T(4,128)} %bitcast.10, f32[4,256,1024]{2,1,0:T(8,128)} %bitcast.7, f32[32,256]{1,0:T(8,128)} %inv.1, f32[256,1024]{1,0:T(8,128)} %bitcast.8, f32[256,256]{1,0:T(8,128)} %bitcast.9, f32[8,256,1024]{2,1,0:T(8,128)} %bitcast.6), custom_call_target="tpu_custom_call" | custom-call | tf_op jit(solution)/shard_map/pallas_call | solution.py:368
  132.3 2.3 %shard_map.78 = (f32[256,1024]{1,0:T(8,128)}, f32[32,1024]{1,0:T(8,128)}) custom-call(f32[256,1024]{1,0:T(8,128)} %get-tuple-element.6.solved, f32[32,1024]{1,0:T(8,128)} %get-tuple-element.7.leaf), custom_call_target="tpu_custom_call" | custom-call | tf_op jit(solution)/shard_map/pallas_call | solution.py:409

commit v3 on v2

--- a/solution.py
+++ b/solution.py
@@ -305,12 +305,17 @@
             s2[rows(8 + s), :] = b
 
         @pl.loop(0, 2)
-        def _(i):
+        def _(n):
+            i = lax.rem(yo // 2 + n, 2)
             v = dot2(ft2[i], s2[...])
             t_all[t, 2 * i] = dot1(it2[2 * i], pair_of(v[:BS]))
             t_all[t, 2 * i + 1] = dot1(it2[2 * i + 1], pair_of(v[BS:]))
 
-        start(t, YXA, YXB, YMB, YPA)
+            @pl.when(n == 0)
+            def _():
+                start(t, YXA, YXB)
+
+        start(t, YMB, YPA)
 
     def y_stage2(t):
         arrived(t, YXA)

time: 135 us -> 134 us (level)
  no operation moved by 1% of the time
where the time goes in v3:
time: 134 us; the launch traced here: 133 us
  Pallas kernels  133 us (99%)
    pallas_call x1, Pallas kernels, body(): pl.pallas_call(kernel, out_shape=(jax.ShapeDtypeStruct((BS, N * W), F32),...  130 us

profile of v3, /device:TPU:2, one launch (start us, length us, event | category | flops | bytes accessed | tf_op | source)
XLA Modules:
  0.0 133.4 jit_solution(9688984130507655242)
XLA Ops:
  0.6 130.5 %shard_map.77 = (f32[256,1024]{1,0:T(8,128)}, f32[32,1024]{1,0:T(8,128)}) custom-call(s32[1,4,8]{2,1,0:T(4,128)} %bitcast.10, f32[4,256,1024]{2,1,0:T(8,128)} %bitcast.7, f32[32,256]{1,0:T(8,128)} %inv.1, f32[256,1024]{1,0:T(8,128)} %bitcast.8, f32[256,256]{1,0:T(8,128)} %bitcast.9, f32[8,256,1024]{2,1,0:T(8,128)} %bitcast.6), custom_call_target="tpu_custom_call" | custom-call | tf_op jit(solution)/shard_map/pallas_call | solution.py:373
  131.1 2.3 %shard_map.78 = (f32[256,1024]{1,0:T(8,128)}, f32[32,1024]{1,0:T(8,128)}) custom-call(f32[256,1024]{1,0:T(8,128)} %get-tuple-element.6.solved, f32[32,1024]{1,0:T(8,128)} %get-tuple-element.7.leaf), custom_call_target="tpu_custom_call" | custom-call | tf_op jit(solution)/shard_map/pallas_call | solution.py:414

commit v4 on v3

--- a/solution.py
+++ b/solution.py
@@ -16,6 +16,8 @@
 
 (PAIR, XA, XB, MB, MA, PA, PB, GP, GM, GC, HA, HBK, FM, FP, FO, YXA, YXB, YMB, YMA, YPA, YPB, Z1) = range(22)
 KINDS = Z1 + 7
+SHARED = {MB: MA, PB: PA, YMB: YMA, YPB: YPA, FM: GC, FP: GC, FO: GC}
+SHARED.update({Z1 + j: Z1 for j in range(1, 7)})
 
 
 def split(v):
@@ -78,9 +80,11 @@
         return pl.ds(pl.multiple_of(at * BS + start, HB), size)
 
     def copy(kind, t):
+        sem = SHARED.get(kind, kind)
+
         def go(src, dst, dev):
             return pltpu.make_async_remote_copy(
-                src_ref=src, dst_ref=dst, send_sem=send.at[t, kind], recv_sem=recv.at[t, kind],
+                src_ref=src, dst_ref=dst, send_sem=send.at[t, sem], recv_sem=recv.at[t, sem],
                 device_id=dev, device_id_type=MESH,
             )
 
@@ -129,9 +133,24 @@
         for kind in kinds:
             copy(kind, t).start()
 
+    def whole(kind, t):
+        ref = None
+        if kind in (MA, PA, YMA, YPA):
+            ref = {MA: ym, PA: yp, YMA: yym, YPA: yyp}[kind].at[t]
+        if kind == GC:
+            ref = s_all.at[t, pl.ds((1 - k) * 4, 4)]
+        if kind == Z1:
+            ref = zr.at[t]
+        if ref is None:
+            return copy(kind, t)
+        return pltpu.make_async_remote_copy(
+            src_ref=ref, dst_ref=ref, send_sem=send.at[t, kind], recv_sem=recv.at[t, kind],
+            device_id=dev_c, device_id_type=MESH,
+        )
+
     def arrived(t, *kinds):
         for kind in kinds:
-            copy(kind, t).wait_recv()
+            whole(kind, t).wait_recv()
 
     def load_f(i):
         return pltpu.make_async_copy(
@@ -278,7 +297,7 @@
         return pltpu.make_async_copy(s_all.at[t, own + x], out_p.at[:, pl.ds(t * W, W)], out_sem.at[t])
 
     def solve(t):
-        arrived(t, MA, MB, PA, PB)
+        arrived(t, MA, PA)
         v = res[t] - ((u_all[t, k, rows(x)] + ym[t]) + yp[t])
         v = dot1(p2[...], pair_of(v))
         s_all[t, own + x] = dot1(pt2[...], pair_of(v))
@@ -296,7 +315,7 @@
         start(t, FO)
 
     def backward(t):
-        arrived(t, GC, FM, FP, FO)
+        arrived(t, GC)
 
         @pl.loop(0, 8)
         def _(s):
@@ -326,19 +345,20 @@
         start(t, YPB)
 
     def z_send(t):
-        arrived(t, YMA, YMB, YPA, YPB)
+        arrived(t, YMA, YPA)
         t_all[t, y] = (t_all[t, y] + yym[t]) + yyp[t]
         start(t, *range(Z1, Z1 + 7))
 
     def finish(t):
-        arrived(t, *range(Z1, Z1 + 7))
+        arrived(t, Z1)
         total = t_all[t, y, mine]
         for j in range(7):
             total = total + zr[t, j]
         out_l[:, pl.ds(pl.multiple_of(t * W, W), W)] = d_all[t] - total
         keep(t).wait()
         for kind in range(KINDS):
-            copy(kind, t).wait_send()
+            if kind not in SHARED:
+                whole(kind, t).wait_send()
 
     stages = dict(
         forward=forward, stage1=stage1, stage2=stage2, solve=solve, relay=relay, opposite=opposite,

time: 134 us -> 134 us (level)
  no operation moved by 1% of the time
where the time goes in v4:
time: 134 us; the launch traced here: 133 us
  Pallas kernels  133 us (99%)
    pallas_call x1, Pallas kernels, body(): pl.pallas_call(kernel, out_shape=(jax.ShapeDtypeStruct((BS, N * W), F32),...  130 us

profile of v4, /device:TPU:2, one launch (start us, length us, event | category | flops | bytes accessed | tf_op | source)
XLA Modules:
  0.0 133.3 jit_solution(18373445357450095764)
XLA Ops:
  0.6 130.4 %shard_map.77 = (f32[256,1024]{1,0:T(8,128)}, f32[32,1024]{1,0:T(8,128)}) custom-call(s32[1,4,8]{2,1,0:T(4,128)} %bitcast.10, f32[4,256,1024]{2,1,0:T(8,128)} %bitcast.7, f32[32,256]{1,0:T(8,128)} %inv.1, f32[256,1024]{1,0:T(8,128)} %bitcast.8, f32[256,256]{1,0:T(8,128)} %bitcast.9, f32[8,256,1024]{2,1,0:T(8,128)} %bitcast.6), custom_call_target="tpu_custom_call" | custom-call | tf_op jit(solution)/shard_map/pallas_call | solution.py:393
  131.0 2.3 %shard_map.78 = (f32[256,1024]{1,0:T(8,128)}, f32[32,1024]{1,0:T(8,128)}) custom-call(f32[256,1024]{1,0:T(8,128)} %get-tuple-element.6.solved, f32[32,1024]{1,0:T(8,128)} %get-tuple-element.7.leaf), custom_call_target="tpu_custom_call" | custom-call | tf_op jit(solution)/shard_map/pallas_call | solution.py:434
